TPU v7x, 256 devices: a whole 4x4x8 slice. The times are simulated.
256 devices in a mesh: ctx: 64 (over y, z, core), head: 4 (over x).
Axes of the slice: x: 4, y: 4, z: 8, core: 2. Of those that a mesh axis runs over, the one named last changes fastest.
Arguments:
- tokens: bfloat16 [32768, 5120], P('ctx', 'head'), may hold values from -48 to 48
- w_query: bfloat16 [5120, 2560], P(None, 'head'), may hold values from -0.078125 to 0.078125
- key_value_weight: bfloat16 [5120, 2, 512], P(None, None, 'head'), may hold values from -0.078125 to 0.078125
- bias_query: float32 [2560], P('head'), may hold values from -3 to 3
- key_value_bias: float32 [2, 512], P(None, 'head'), may hold values from -3 to 3
- destination: int32 [4096], replicated, may hold values from 0 to 4095, as said below
- doc_ids: int32 [4096], replicated, may hold values from 0 to 127, never falling along the last dimension, each value on 1 to 384 neighbouring positions
Outputs:
- attended: bfloat16 [32768, 2560], P('ctx', 'head')
Inputs may be any that keep to these rules, and one draw needn't show every extreme that they name: A permutation of the 4096 blocks: old block b, held by ctx index b // 64, goes to ctx index destination[b] // 64. The blocks of each old holder go to exactly 64 new holders, 1 to each. `doc_ids`: Non-decreasing; each document covers 1 to 384 consecutive blocks.
All inputs are finite; a program needn't handle non-finite values.
Results may differ from a plain program's by a relative error of at most 0.012.
The roundings to bfloat16 on the way count: a program that leaves them out, or rounds other values in their place, can miss the bound.
Values may be sent and summed in bfloat16 or wider, within the bound.
A program may use at most 64 MiB of HBM per device.

v0:
```python
import functools
import math

import jax
import jax.numpy as jnp
from jax import lax
from jax.experimental import pallas as pl
from jax.experimental.pallas import tpu as pltpu
from jax.sharding import PartitionSpec as P

MESH = pl.DeviceIdType.MESH
HEAD_SIZE = 128
HEADS = 5
BLOCK = 8
Y, Z, C, X = 4, 8, 2, 4
N = Y * Z * C
G = 4
PER = N // G
ROWS = PER * BLOCK
SHARD = N * BLOCK
HALF = 640
DEPTH = 2 * HALF
QW = HEADS * HEAD_SIZE
DISTANCES = (0, 2, 4, 6, 1, 3, 5)
NBUF = len(DISTANCES)
KEYS = NBUF * ROWS
NEG = -1e30
SCALE = 1.0 / math.sqrt(HEAD_SIZE) * math.log2(math.e)


def offset_of(slot):
    g, r = slot // PER, slot % PER
    dz, dc = r // C, r % C
    return (g + dz) % Y, dz, dc


def moved(ctx, offset, sign):
    dy, dz, dc = offset
    y, z, c = ctx // (Z * C), (ctx // C) % Z, ctx % C
    y = (y + sign * dy + Y) % Y
    z = (z + sign * dz + Z) % Z
    c = (c + sign * dc + C) % C
    return (y * Z + z) * C + c


def kernel(pick, inv, kpos, qlo, qhi, bq, bkv, tokens, wq_hbm, wkv_hbm, out,
           tok, send, xg, wq, wraw, wkv, acc, qs, kv, pb, m_ref, l_ref, o_ref, on, stage,
           local_sem, a2a_send, a2a_recv, xs_send, x_recv, rl_send, rl_recv,
           kv_send, kv_recv, pb_send, pb_recv):
    me = lax.axis_index("ctx")
    x = lax.axis_index("head")
    core = lax.rem(me, C)
    right, left = lax.rem(x + 1, X), lax.rem(x + X - 1, X)
    onward = lax.rem(me + C, N)
    partner = me + 1 - 2 * core

    load_tok = pltpu.make_async_copy(tokens, tok, local_sem.at[0])
    load_wq = pltpu.make_async_copy(wq_hbm, wq, local_sem.at[1])
    load_wkv = pltpu.make_async_copy(wkv_hbm, wraw, local_sem.at[2])
    load_tok.start()
    load_wkv.start()
    load_wq.start()

    barrier = pltpu.get_barrier_semaphore()

    @pl.loop(1, N)
    def _(s):
        pl.semaphore_signal(barrier, inc=1, device_id=(moved(me, offset_of(s), 1), x), device_id_type=MESH)

    pl.semaphore_signal(barrier, inc=1, device_id=(me, right), device_id_type=MESH)
    pl.semaphore_signal(barrier, inc=1, device_id=(me, left), device_id_type=MESH)

    load_tok.wait()

    @pl.loop(0, N)
    def _(s):
        rows = tok[pick[s]].astype(jnp.float32)
        both = jnp.concatenate([rows[:, :HALF], rows[:, HALF:]], axis=0)
        send[s] = both.astype(jnp.bfloat16)

    pl.semaphore_wait(barrier, N + 1)

    def a2a(s, g):
        return pltpu.make_async_remote_copy(
            src_ref=send.at[s], dst_ref=xg.at[0, s], send_sem=a2a_send, recv_sem=a2a_recv.at[g],
            device_id=(moved(me, offset_of(s), 1), x), device_id_type=MESH)

    own = pltpu.make_async_copy(send.at[0], xg.at[0, 0], a2a_recv.at[0])
    own.start()

    @pl.loop(1, N)
    def _(s):
        a2a(s, s // PER).start()

    def group(g):
        return pl.ds(g * PER, PER)

    def x_send(g, side):
        return pltpu.make_async_remote_copy(
            src_ref=xg.at[0, group(g)], dst_ref=xg.at[1 + side, group(g)],
            send_sem=xs_send.at[side, g], recv_sem=x_recv.at[side, g],
            device_id=(me, right if side == 0 else left), device_id_type=MESH)

    def relay(g, side):
        half = pl.ds(g * PER + side * (PER // 2), PER // 2)
        return pltpu.make_async_remote_copy(
            src_ref=xg.at[1 + side, half], dst_ref=xg.at[3, half],
            send_sem=rl_send.at[side, g], recv_sem=rl_recv.at[side, g],
            device_id=(me, right if side == 0 else left), device_id_type=MESH)

    def kv_copy(g, h):
        return pltpu.make_async_remote_copy(
            src_ref=kv.at[h, g], dst_ref=kv.at[h + 1, g],
            send_sem=kv_send.at[h, g], recv_sem=kv_recv.at[h, g],
            device_id=(onward, x), device_id_type=MESH)

    def pb_copy(g, i):
        return pltpu.make_async_remote_copy(
            src_ref=kv.at[i + core, g], dst_ref=pb.at[i, g],
            send_sem=pb_send.at[i, g], recv_sem=pb_recv.at[i, g],
            device_id=(partner, x), device_id_type=MESH)

    def group_ready(g):
        pltpu.make_async_copy(xg.at[0, group(g)], xg.at[0, group(g)], a2a_recv.at[g]).wait()
        x_send(g, 0).start()
        x_send(g, 1).start()

    def chain(g, h):
        kv_copy(g, h - 1).wait_recv()
        if h < 3:
            kv_copy(g, h).start()
        pb_copy(g, h - 1).start()

    def chain_end(g):
        for i in range(3):
            pb_copy(g, i).wait_recv()

    load_wkv.wait()

    @pl.loop(0, 20)
    def _(t):
        raw = wraw[pl.ds(t * 512, 512), :].astype(jnp.float32)
        stage[...] = raw
        rows = pl.ds(t * 256, 256)
        wkv[rows, :HEAD_SIZE] = stage[pl.ds(0, 256, 2), :].astype(jnp.bfloat16)
        wkv[rows, HEAD_SIZE:] = stage[pl.ds(1, 256, 2), :].astype(jnp.bfloat16)

    m_ref[...] = jnp.full_like(m_ref, NEG)
    l_ref[...] = jnp.zeros_like(l_ref)
    o_ref[...] = jnp.zeros_like(o_ref)

    def project_part(g, part, peer):
        piece = xg[part, group(g)].astype(jnp.float32)
        lhs = jnp.concatenate(
            [piece[:, :BLOCK].reshape(ROWS, HALF), piece[:, BLOCK:].reshape(ROWS, HALF)], axis=1
        ).astype(jnp.bfloat16)
        depth = pl.ds(pl.multiple_of(peer * DEPTH, DEPTH), DEPTH)
        acc[:, :QW] += jnp.dot(lhs, wq[depth, :], preferred_element_type=jnp.float32)
        acc[:, QW:] += jnp.dot(lhs, wkv[depth, :], preferred_element_type=jnp.float32)

    def project(g):
        acc[...] = jnp.concatenate(
            [jnp.broadcast_to(bq[...], (ROWS, QW)),
             jnp.broadcast_to(bkv[0:1, :], (ROWS, HEAD_SIZE)),
             jnp.broadcast_to(bkv[1:2, :], (ROWS, HEAD_SIZE))], axis=1)

        @pl.loop(0, 4)
        def _(part):
            @pl.when(part == 3)
            def _():
                relay(g, 0).wait_recv()
                relay(g, 1).wait_recv()

            shift = jnp.where(part == 3, 2, jnp.where(part == 1, X - 1, jnp.where(part == 2, 1, 0)))
            project_part(g, part, lax.rem(x + shift, X))

        for h in range(HEADS):
            qs[g, pl.ds(h * ROWS, ROWS), :] = acc[:, h * HEAD_SIZE:(h + 1) * HEAD_SIZE].astype(jnp.bfloat16)
        kv[0, g] = acc[:, QW:].astype(jnp.bfloat16)
        kv_copy(g, 0).start()

    def attend(i, j):
        keys = jnp.concatenate(
            [kv[h, j][:, :HEAD_SIZE] for h in range(4)] + [pb[h, j][:, :HEAD_SIZE] for h in range(3)], axis=0)
        values = jnp.concatenate(
            [kv[h, j][:, HEAD_SIZE:] for h in range(4)] + [pb[h, j][:, HEAD_SIZE:] for h in range(3)], axis=0)
        place = kpos[j]
        bias = jnp.where((place <= qhi[i]) & (place >= qlo[i]), 0.0, NEG)
        s = lax.dot_general(qs[i], keys, (((1,), (1,)), ((), ())), preferred_element_type=jnp.float32)
        s = (s.reshape(HEADS, ROWS, KEYS) + bias[None]).reshape(HEADS * ROWS, KEYS)
        m_old = m_ref[i]
        m_new = jnp.maximum(m_old, jnp.max(s, axis=1, keepdims=True))
        p = jnp.exp2((s - m_new[:, :1]) * SCALE)
        alpha = jnp.exp2((m_old - m_new) * SCALE)
        l_ref[i] = l_ref[i] * alpha + jnp.sum(p, axis=1, keepdims=True)
        o_ref[i] = o_ref[i] * alpha + jnp.dot(p.astype(jnp.bfloat16), values, preferred_element_type=jnp.float32)
        m_ref[i] = m_new

    group_ready(0)
    load_wq.wait()

    @pl.loop(0, G + 2)
    def _(step):
        @pl.when(step >= 2)
        def _():
            j = step - 2
            chain_end(j)
            rows_there = jnp.minimum(step, G)
            older = jnp.where(step <= G, j, 0)

            @pl.loop(0, rows_there + older)
            def _(t):
                i = jnp.where(t < rows_there, t, rows_there - 1)
                jj = jnp.where(t < rows_there, j, t - rows_there)
                attend(i, jj)

        @pl.when(step < G)
        def _():
            x_send(step, 0).wait_recv()
            relay(step, 0).start()
            x_send(step, 1).wait_recv()
            relay(step, 1).start()

        @pl.when(step + 1 < G)
        def _():
            group_ready(step + 1)

        @pl.when((step >= 1) & (step <= G))
        def _():
            chain(step - 1, 1)

        @pl.when(step < G)
        def _():
            project(step)

        @pl.when((step >= 1) & (step <= G))
        def _():
            chain(step - 1, 2)
            chain(step - 1, 3)

    @pl.loop(0, G)
    def _(g):
        for h in range(HEADS):
            rows = pl.ds(h * ROWS, ROWS)
            part = o_ref[g, rows, :] / l_ref[g, rows, :]
            on[pl.ds(h * N + g * PER, PER)] = part.reshape(PER, BLOCK, HEAD_SIZE)

    @pl.loop(0, N // 2)
    def _(t):
        first, second = inv[2 * t], inv[2 * t + 1]
        rows = pl.ds(t * 2 * BLOCK, 2 * BLOCK)
        for h in range(HEADS):
            pair = jnp.concatenate([on[h * N + first], on[h * N + second]], axis=0)
            out[rows, h * HEAD_SIZE:(h + 1) * HEAD_SIZE] = pair.astype(jnp.bfloat16)

    pltpu.make_async_copy(send.at[pl.ds(1, N - 1)], send.at[pl.ds(1, N - 1)], a2a_send).wait()

    @pl.loop(0, G)
    def _(g):
        for side in range(2):
            x_send(g, side).wait_send()
            relay(g, side).wait_send()
        for h in range(3):
            kv_copy(g, h).wait_send()
            pb_copy(g, h).wait_send()


def per_device(tokens, w_query, key_value_weight, bias_query, key_value_bias, destination, doc_ids):
    me = lax.axis_index("ctx")
    slots = jnp.arange(N, dtype=jnp.int32)
    table = destination.reshape(N, N)
    target = moved(me, offset_of(slots), 1)
    mine = lax.dynamic_slice_in_dim(table, me, 1)[0]
    pick = jnp.sum(jnp.where((mine // N)[None, :] == target[:, None], slots[None, :], 0), axis=1)
    shards = me - jnp.array(DISTANCES, jnp.int32)
    wrapped = (shards + N) % N
    place = jnp.sum(jnp.where((table // N)[None] == wrapped[:, None, None], (table % N)[None], 0), axis=2)
    senders = jnp.stack(
        [moved(wrapped[d], offset_of(slots), -1) for d in range(NBUF)])
    in_slot = jnp.sum(jnp.where(senders[:, :, None] == slots[None, None, :], place[:, None, :], 0), axis=2)
    inv = jnp.sum(jnp.where(in_slot[0][None, :] == slots[:, None], slots[None, :], 0), axis=1)
    lanes = jnp.arange(BLOCK, dtype=jnp.int32)
    token_at = shards[:, None, None] * SHARD + in_slot[:, :, None] * BLOCK + lanes
    kpos = token_at.reshape(NBUF, G, ROWS).transpose(1, 0, 2).reshape(G, 1, KEYS)
    qhi = token_at[0].reshape(G, ROWS, 1)
    docs = lax.dynamic_slice_in_dim(doc_ids, me * N, N)
    starts = jnp.sum((doc_ids[None, :] < docs[:, None]).astype(jnp.int32), axis=1) * BLOCK
    start_in_slot = jnp.sum(jnp.where(in_slot[0][:, None] == slots[None, :], starts[None, :], 0), axis=1)
    qlo = jnp.broadcast_to(start_in_slot[:, None], (N, BLOCK)).reshape(G, ROWS, 1)

    vmem, smem, hbm = (pl.BlockSpec(memory_space=s) for s in (pltpu.VMEM, pltpu.SMEM, pl.ANY))
    bf16, f32 = jnp.bfloat16, jnp.float32
    dma = pltpu.SemaphoreType.DMA
    return pl.pallas_call(
        kernel,
        out_shape=jax.ShapeDtypeStruct((SHARD, QW), bf16),
        in_specs=[smem, smem, vmem, vmem, vmem, vmem, vmem, hbm, hbm, hbm],
        out_specs=vmem,
        scratch_shapes=[
            pltpu.VMEM((N, BLOCK, DEPTH), bf16),
            pltpu.VMEM((N, 2 * BLOCK, HALF), bf16),
            pltpu.VMEM((X, N, 2 * BLOCK, HALF), bf16),
            pltpu.VMEM((X * DEPTH, QW), bf16),
            pltpu.VMEM((2 * X * DEPTH, HEAD_SIZE), bf16),
            pltpu.VMEM((X * DEPTH, 2 * HEAD_SIZE), bf16),
            pltpu.VMEM((ROWS, QW + 2 * HEAD_SIZE), f32),
            pltpu.VMEM((G, HEADS * ROWS, HEAD_SIZE), bf16),
            pltpu.VMEM((4, G, ROWS, 2 * HEAD_SIZE), bf16),
            pltpu.VMEM((3, G, ROWS, 2 * HEAD_SIZE), bf16),
            pltpu.VMEM((G, HEADS * ROWS, HEAD_SIZE), f32),
            pltpu.VMEM((G, HEADS * ROWS, HEAD_SIZE), f32),
            pltpu.VMEM((G, HEADS * ROWS, HEAD_SIZE), f32),
            pltpu.VMEM((HEADS * N, BLOCK, HEAD_SIZE), f32),
            pltpu.VMEM((512, HEAD_SIZE), f32),
            dma((3,)), dma, dma((G,)),
            dma((2, G)), dma((2, G)), dma((2, G)), dma((2, G)),
            dma((3, G)), dma((3, G)), dma((3, G)), dma((3, G)),
        ],
        compiler_params=pltpu.CompilerParams(
            collective_id=0, has_side_effects=True, vmem_limit_bytes=56 * 1024 * 1024),
    )(pick, inv, kpos, qlo, qhi, bias_query.reshape(1, QW), key_value_bias,
      tokens.reshape(N, BLOCK, DEPTH), w_query, key_value_weight.reshape(2 * X * DEPTH, HEAD_SIZE))


def solution(mesh):
    placed = (
        P("ctx", "head"),
        P(None, "head"),
        P(None, None, "head"),
        P("head"),
        P(None, "head"),
        P(),
        P(),
    )
    return jax.shard_map(
        per_device, mesh=mesh, in_specs=placed, out_specs=P("ctx", "head"), check_vma=False
    )
```

profile of v0, /device:TPU:1, one launch (start us, length us, event | category | flops | bytes accessed | tf_op | source)
XLA Modules:
  0.0 151.8 jit_solution(1694276714405597637)
XLA Ops:
  0.0 0.8 dynamic_slice.7
  0.8 1.0 convert_reduce_fusion
  1.8 0.7 add_multiply_fusion
  2.5 1.3 reshape.1278.bq
  3.7 0.7 fusion.62
  22.5 0.1 add.1588
  22.6 0.8 reshape.1276
  23.4 0.8 select_reduce_fusion.4.pick
  24.2 0.3 select_reduce_fusion.1
  24.5 0.3 select_reduce_fusion
  24.8 0.1 multiply_add_fusion
  24.9 0.7 select_reduce_fusion.2
  25.5 0.1 broadcast_in_dim.84
  25.6 0.1 broadcast_in_dim.85
  25.7 0.1 iota_add_fusion
  25.8 0.1 add.1585
  25.9 0.1 add.1586
  26.1 0.6 copy.13.kpos
  26.7 0.8 reshape_squeeze.4.qhi
  27.5 0.8 broadcast_in_dim.87.qlo
  28.3 121.5 %shard_map.82 = bf16[512,640]{1,0:T(8,128)(2,1)} custom-call(s32[64]{0:T(128)} %select_reduce_fusion.4.pick, s32[64]{0:T(128)} %get-tuple-element.6.inv, s32[4,1,896]{2,1,0:T(1,128)} %copy.13.kpos, s32[4,128,1]{2,1,0:T(8,128)} %broadcast_in_dim.87.qlo, s32[4,128,1]{2,1,0:T(8,128)} %reshape_squeeze.4.qhi, f32[1,640]{1,0:T(1,128)} %reshape.1278.bq, ...), custom_call_target="tpu_custom_call" | custom-call | tf_op jit(solution)/shard_map/pallas_call | solution.py:294
  149.8 2.0 %copy.17 = bf16[512,640]{1,0:T(8,128)(2,1)} copy(bf16[512,640]{1,0:T(8,128)(2,1)} %shard_map.82) | data formatting | bytes 1310720
  (13 shorter events, 0.2 us)
where the time goes:
time: 152 us
  Pallas kernels  121 us (80%)
  between operations  18 us (12%)
  local copies, waits for them, and re-layouts  8.29 us (5%)
  other arithmetic  4.04 us (3%)
    pallas_call x1, Pallas kernels, per_device(): pl.pallas_call(kernel, out_shape=jax.ShapeDtypeStruct((SHARD, QW), bf16),...  121 us

commit v1 on v0

--- a/solution.py
+++ b/solution.py
@@ -28,28 +28,34 @@
 SCALE = 1.0 / math.sqrt(HEAD_SIZE) * math.log2(math.e)
 
 
-def offset_of(slot):
-    g, r = slot // PER, slot % PER
-    dz, dc = r // C, r % C
-    return (g + dz) % Y, dz, dc
-
-
-def moved(ctx, offset, sign):
-    dy, dz, dc = offset
-    y, z, c = ctx // (Z * C), (ctx // C) % Z, ctx % C
-    y = (y + sign * dy + Y) % Y
-    z = (z + sign * dz + Z) % Z
-    c = (c + sign * dc + C) % C
-    return (y * Z + z) * C + c
-
-
-def kernel(pick, inv, kpos, qlo, qhi, bq, bkv, tokens, wq_hbm, wkv_hbm, out,
+def slot_parts(slot):
+    dz, dc = (slot >> 1) & (Z - 1), slot & 1
+    return ((slot >> 4) + dz) & (Y - 1), dz, dc
+
+
+def sender_of(ctx, slot):
+    dy, dz, dc = slot_parts(slot)
+    return ((((ctx >> 4) - dy) & (Y - 1)) << 4) + ((((ctx >> 1) - dz) & (Z - 1)) << 1) + ((ctx - dc) & 1)
+
+
+def target_of(ctx, slot):
+    dy, dz, dc = slot_parts(slot)
+    return ((((ctx >> 4) + dy) & (Y - 1)) << 4) + ((((ctx >> 1) + dz) & (Z - 1)) << 1) + ((ctx + dc) & 1)
+
+
+def iota(shape, dim):
+    return lax.broadcasted_iota(jnp.int32, shape, dim)
+
+
+def kernel(table, docs, bq, bkv, tokens, wq_hbm, wkv_hbm, out,
            tok, send, xg, wq, wraw, wkv, acc, qs, kv, pb, m_ref, l_ref, o_ref, on, stage,
+           kpos, qlo, qhi, qplace,
            local_sem, a2a_send, a2a_recv, xs_send, x_recv, rl_send, rl_recv,
            kv_send, kv_recv, pb_send, pb_recv):
     me = lax.axis_index("ctx")
     x = lax.axis_index("head")
     core = lax.rem(me, C)
+    my_y, my_z = lax.div(me, Z * C), lax.rem(lax.div(me, C), Z)
     right, left = lax.rem(x + 1, X), lax.rem(x + X - 1, X)
     onward = lax.rem(me + C, N)
     partner = me + 1 - 2 * core
@@ -63,34 +69,53 @@
 
     barrier = pltpu.get_barrier_semaphore()
 
-    @pl.loop(1, N)
-    def _(s):
-        pl.semaphore_signal(barrier, inc=1, device_id=(moved(me, offset_of(s), 1), x), device_id_type=MESH)
+    def chip_at(u):
+        g, dz = lax.div(u, Z), lax.rem(u, Z)
+        return (lax.rem(my_y + lax.rem(g + dz, Y), Y) * Z + lax.rem(my_z + dz, Z)) * C
+
+    def cores_at(u):
+        chip = chip_at(u)
+        return (2 * u, chip + core), (2 * u + 1, chip + 1 - core)
+
+    pl.semaphore_signal(barrier, inc=1, device_id=(partner, x), device_id_type=MESH)
+
+    @pl.loop(1, N // 2)
+    def _(u):
+        for _, target in cores_at(u):
+            pl.semaphore_signal(barrier, inc=1, device_id=(target, x), device_id_type=MESH)
 
     pl.semaphore_signal(barrier, inc=1, device_id=(me, right), device_id_type=MESH)
     pl.semaphore_signal(barrier, inc=1, device_id=(me, left), device_id_type=MESH)
 
+    shift = (me & 1) * N
+    mine = table[pl.ds(lax.div(me, 2), 1), :]
+    spread = jnp.where(iota((128, SHARD), 0) == shift + (iota((128, SHARD), 1) >> 3), 1.0, 0.0).astype(jnp.bfloat16)
+    owners = jnp.broadcast_to((mine >> 6).astype(jnp.float32).astype(jnp.bfloat16), (8, 128))
+    owner_of = jnp.dot(owners, spread, preferred_element_type=jnp.float32)[0:1].astype(jnp.int32)
     load_tok.wait()
-
-    @pl.loop(0, N)
-    def _(s):
-        rows = tok[pick[s]].astype(jnp.float32)
-        both = jnp.concatenate([rows[:, :HALF], rows[:, HALF:]], axis=0)
-        send[s] = both.astype(jnp.bfloat16)
+    for g in range(G):
+        row = iota((ROWS, 1), 0)
+        target = target_of(me, (row >> 3) + g * PER)
+        pick = (owner_of == target) & ((iota((1, SHARD), 1) & 7) == (row & 7))
+        picked = jnp.dot(jnp.where(pick, 1.0, 0.0).astype(jnp.bfloat16), tok[...], preferred_element_type=jnp.float32)
+        halves = [picked[:, h * HALF:(h + 1) * HALF].reshape(PER, BLOCK, HALF) for h in range(2)]
+        send[pl.ds(g * PER, PER)] = jnp.concatenate(halves, axis=1).astype(jnp.bfloat16)
 
     pl.semaphore_wait(barrier, N + 1)
 
-    def a2a(s, g):
-        return pltpu.make_async_remote_copy(
-            src_ref=send.at[s], dst_ref=xg.at[0, s], send_sem=a2a_send, recv_sem=a2a_recv.at[g],
-            device_id=(moved(me, offset_of(s), 1), x), device_id_type=MESH)
+    def a2a(s, target):
+        return pltpu.make_async_remote_copy(
+            src_ref=send.at[s], dst_ref=xg.at[0, s], send_sem=a2a_send, recv_sem=a2a_recv.at[lax.div(s, PER)],
+            device_id=(target, x), device_id_type=MESH)
 
     own = pltpu.make_async_copy(send.at[0], xg.at[0, 0], a2a_recv.at[0])
     own.start()
-
-    @pl.loop(1, N)
-    def _(s):
-        a2a(s, s // PER).start()
+    a2a(1, partner).start()
+
+    @pl.loop(1, N // 2)
+    def _(u):
+        for s, target in cores_at(u):
+            a2a(s, target).start()
 
     def group(g):
         return pl.ds(g * PER, PER)
@@ -144,6 +169,50 @@
         rows = pl.ds(t * 256, 256)
         wkv[rows, :HEAD_SIZE] = stage[pl.ds(0, 256, 2), :].astype(jnp.bfloat16)
         wkv[rows, HEAD_SIZE:] = stage[pl.ds(1, 256, 2), :].astype(jnp.bfloat16)
+
+    entry = table[...]
+    entry_place = (entry & (N - 1)).astype(jnp.float32)
+    lane = iota((1, 128), 1)
+    lane_slot = iota((1, SHARD), 1) >> 3
+    lane_token = (iota((1, SHARD), 1) & 7).astype(jnp.float32)
+    pair = iota((N // 2, 1), 0)
+    for buf, distance in enumerate(DISTANCES):
+        shard = me - distance
+        wrapped = shard & (N - 1)
+        found = jnp.where((entry >> 6) == wrapped, entry_place, 0.0)
+        even = jnp.sum(jnp.where(lane < N, found, 0.0), axis=1, keepdims=True)
+        odd = jnp.sum(jnp.where(lane < N, 0.0, found), axis=1, keepdims=True)
+        sender = sender_of(wrapped, lane_slot)
+        hit = (sender >> 1) == pair
+        place = jnp.sum(jnp.where(hit, jnp.where((sender & 1) == 0, even, odd), 0.0), axis=0, keepdims=True)
+        row = (shard * SHARD).astype(jnp.float32) + place * BLOCK + lane_token
+        for g in range(G):
+            kpos[g, 0:1, buf * ROWS:(buf + 1) * ROWS] = row[:, g * ROWS:(g + 1) * ROWS]
+        if buf == 0:
+            mate = (lane >> 1) == pair
+            place_row = jnp.sum(jnp.where(mate, jnp.where((lane & 1) == 0, even, odd), 0.0), axis=0, keepdims=True)
+            row_index = iota((SHARD, 1), 0)
+            mine_from = sender_of(me, row_index >> 3)
+            place_col = jnp.sum(jnp.where(lane == mine_from, place_row, 0.0), axis=1, keepdims=True)
+            position = place_col * BLOCK + (row_index & 7).astype(jnp.float32)
+            qplace[...] = row - (shard * SHARD).astype(jnp.float32)
+            here = (shard * SHARD).astype(jnp.float32) + position
+            for g in range(G):
+                qhi[g] = here[g * ROWS:(g + 1) * ROWS]
+
+    my_docs = docs[pl.ds(lax.div(me, 2), 1), :].astype(jnp.float32)
+    at = iota((N, 1), 0)
+    doc_col = jnp.sum(jnp.where(lane == at + shift, my_docs, 0.0), axis=1, keepdims=True)
+
+    def count(r, total):
+        return total + jnp.where(docs[pl.ds(r, 1), :].astype(jnp.float32) < doc_col, 1.0, 0.0)
+
+    counted = lax.fori_loop(0, 32, count, jnp.zeros((N, 128), jnp.float32))
+    start_col = jnp.sum(counted, axis=1, keepdims=True) * BLOCK
+    start_row = jnp.sum(jnp.where(lane == at, start_col, 0.0), axis=0, keepdims=True)
+    low = jnp.sum(jnp.where(lane.astype(jnp.float32) == place_col, start_row, 0.0), axis=1, keepdims=True)
+    for g in range(G):
+        qlo[g] = low[g * ROWS:(g + 1) * ROWS]
 
     m_ref[...] = jnp.full_like(m_ref, NEG)
     l_ref[...] = jnp.zeros_like(l_ref)
@@ -160,9 +229,7 @@
 
     def project(g):
         acc[...] = jnp.concatenate(
-            [jnp.broadcast_to(bq[...], (ROWS, QW)),
-             jnp.broadcast_to(bkv[0:1, :], (ROWS, HEAD_SIZE)),
-             jnp.broadcast_to(bkv[1:2, :], (ROWS, HEAD_SIZE))], axis=1)
+            [jnp.broadcast_to(b[h:h + 1, :], (ROWS, HEAD_SIZE)) for b in (bq, bkv) for h in range(b.shape[0])], axis=1)
 
         @pl.loop(0, 4)
         def _(part):
@@ -243,15 +310,10 @@
         for h in range(HEADS):
             rows = pl.ds(h * ROWS, ROWS)
             part = o_ref[g, rows, :] / l_ref[g, rows, :]
-            on[pl.ds(h * N + g * PER, PER)] = part.reshape(PER, BLOCK, HEAD_SIZE)
-
-    @pl.loop(0, N // 2)
-    def _(t):
-        first, second = inv[2 * t], inv[2 * t + 1]
-        rows = pl.ds(t * 2 * BLOCK, 2 * BLOCK)
-        for h in range(HEADS):
-            pair = jnp.concatenate([on[h * N + first], on[h * N + second]], axis=0)
-            out[rows, h * HEAD_SIZE:(h + 1) * HEAD_SIZE] = pair.astype(jnp.bfloat16)
+            on[pl.ds(g * ROWS, ROWS), h * HEAD_SIZE:(h + 1) * HEAD_SIZE] = part.astype(jnp.bfloat16)
+
+    order = jnp.where(iota((SHARD, 1), 0).astype(jnp.float32) == qplace[...], 1.0, 0.0).astype(jnp.bfloat16)
+    out[...] = jnp.dot(order, on[...], preferred_element_type=jnp.float32).astype(jnp.bfloat16)
 
     pltpu.make_async_copy(send.at[pl.ds(1, N - 1)], send.at[pl.ds(1, N - 1)], a2a_send).wait()
 
@@ -266,38 +328,16 @@
 
 
 def per_device(tokens, w_query, key_value_weight, bias_query, key_value_bias, destination, doc_ids):
-    me = lax.axis_index("ctx")
-    slots = jnp.arange(N, dtype=jnp.int32)
-    table = destination.reshape(N, N)
-    target = moved(me, offset_of(slots), 1)
-    mine = lax.dynamic_slice_in_dim(table, me, 1)[0]
-    pick = jnp.sum(jnp.where((mine // N)[None, :] == target[:, None], slots[None, :], 0), axis=1)
-    shards = me - jnp.array(DISTANCES, jnp.int32)
-    wrapped = (shards + N) % N
-    place = jnp.sum(jnp.where((table // N)[None] == wrapped[:, None, None], (table % N)[None], 0), axis=2)
-    senders = jnp.stack(
-        [moved(wrapped[d], offset_of(slots), -1) for d in range(NBUF)])
-    in_slot = jnp.sum(jnp.where(senders[:, :, None] == slots[None, None, :], place[:, None, :], 0), axis=2)
-    inv = jnp.sum(jnp.where(in_slot[0][None, :] == slots[:, None], slots[None, :], 0), axis=1)
-    lanes = jnp.arange(BLOCK, dtype=jnp.int32)
-    token_at = shards[:, None, None] * SHARD + in_slot[:, :, None] * BLOCK + lanes
-    kpos = token_at.reshape(NBUF, G, ROWS).transpose(1, 0, 2).reshape(G, 1, KEYS)
-    qhi = token_at[0].reshape(G, ROWS, 1)
-    docs = lax.dynamic_slice_in_dim(doc_ids, me * N, N)
-    starts = jnp.sum((doc_ids[None, :] < docs[:, None]).astype(jnp.int32), axis=1) * BLOCK
-    start_in_slot = jnp.sum(jnp.where(in_slot[0][:, None] == slots[None, :], starts[None, :], 0), axis=1)
-    qlo = jnp.broadcast_to(start_in_slot[:, None], (N, BLOCK)).reshape(G, ROWS, 1)
-
-    vmem, smem, hbm = (pl.BlockSpec(memory_space=s) for s in (pltpu.VMEM, pltpu.SMEM, pl.ANY))
+    vmem, hbm = (pl.BlockSpec(memory_space=s) for s in (pltpu.VMEM, pl.ANY))
     bf16, f32 = jnp.bfloat16, jnp.float32
     dma = pltpu.SemaphoreType.DMA
     return pl.pallas_call(
         kernel,
         out_shape=jax.ShapeDtypeStruct((SHARD, QW), bf16),
-        in_specs=[smem, smem, vmem, vmem, vmem, vmem, vmem, hbm, hbm, hbm],
+        in_specs=[vmem, vmem, vmem, vmem, hbm, hbm, hbm],
         out_specs=vmem,
         scratch_shapes=[
-            pltpu.VMEM((N, BLOCK, DEPTH), bf16),
+            pltpu.VMEM((SHARD, DEPTH), bf16),
             pltpu.VMEM((N, 2 * BLOCK, HALF), bf16),
             pltpu.VMEM((X, N, 2 * BLOCK, HALF), bf16),
             pltpu.VMEM((X * DEPTH, QW), bf16),
@@ -310,16 +350,20 @@
             pltpu.VMEM((G, HEADS * ROWS, HEAD_SIZE), f32),
             pltpu.VMEM((G, HEADS * ROWS, HEAD_SIZE), f32),
             pltpu.VMEM((G, HEADS * ROWS, HEAD_SIZE), f32),
-            pltpu.VMEM((HEADS * N, BLOCK, HEAD_SIZE), f32),
+            pltpu.VMEM((SHARD, QW), bf16),
             pltpu.VMEM((512, HEAD_SIZE), f32),
+            pltpu.VMEM((G, 1, KEYS), f32),
+            pltpu.VMEM((G, ROWS, 1), f32),
+            pltpu.VMEM((G, ROWS, 1), f32),
+            pltpu.VMEM((1, SHARD), f32),
             dma((3,)), dma, dma((G,)),
             dma((2, G)), dma((2, G)), dma((2, G)), dma((2, G)),
             dma((3, G)), dma((3, G)), dma((3, G)), dma((3, G)),
         ],
         compiler_params=pltpu.CompilerParams(
             collective_id=0, has_side_effects=True, vmem_limit_bytes=56 * 1024 * 1024),
-    )(pick, inv, kpos, qlo, qhi, bias_query.reshape(1, QW), key_value_bias,
-      tokens.reshape(N, BLOCK, DEPTH), w_query, key_value_weight.reshape(2 * X * DEPTH, HEAD_SIZE))
+    )(destination.reshape(N // 2, 128), doc_ids.reshape(N // 2, 128), bias_query.reshape(HEADS, HEAD_SIZE), key_value_bias,
+      tokens, w_query, key_value_weight.reshape(2 * X * DEPTH, HEAD_SIZE))
 
 
 def solution(mesh):

time: 152 us -> 122 us (0.80)
  between operations: 18 us -> 0.01 us
  local copies, waits for them, and re-layouts: 8.29 us -> 1.98 us
  other arithmetic: 4.04 us -> 0 us
    reduce_sum x5 -> x0, other arithmetic: 3.01 us -> none  [the longest x1 0.99 us: per_device(): jnp.sum((doc_ids[None, :] < docs[:, None]).astype(jnp.int32), axis=1)]
    reshape x3 -> x0, local copies, waits for them, and re-layouts: 2.67 us -> none  [the longest x1 1.27 us: per_device(): bias_query.reshape(1, QW)]
    pallas_call x1, Pallas kernels: 121 us -> 120 us  [per_device(): pl.pallas_call(kernel, out_shape=jax.ShapeDtypeStruct((SHARD, QW), bf16),...]
where the time goes in v1:
time: 122 us
  Pallas kernels  120 us (98%)
  local copies, waits for them, and re-layouts  1.98 us (2%)
    pallas_call x1, Pallas kernels, per_device(): pl.pallas_call(kernel, out_shape=jax.ShapeDtypeStruct((SHARD, QW), bf16),...  120 us

profile of v1, /device:TPU:1, one launch (start us, length us, event | category | flops | bytes accessed | tf_op | source)
XLA Modules:
  0.0 121.6 jit_solution(17489035123950759167)
XLA Ops:
  0.0 119.7 %shard_map.73 = bf16[512,640]{1,0:T(8,128)(2,1)} custom-call(s32[32,128]{1,0:T(8,128)} %bitcast.5, s32[32,128]{1,0:T(8,128)} %bitcast.6, f32[5,128]{1,0:T(8,128)} %bitcast.7, f32[2,128]{1,0:T(2,128)} %bkv.1, bf16[512,1280]{1,0:T(8,128)(2,1)} %tokens.1, bf16[5120,640]{1,0:T(8,128)(2,1)} %wq_hbm.1, bf16[10240,128]{1,0:T(8,128)(2,1)} %bitcast.4), custom_call_target="tpu_custom_call" | custom-call | tf_op jit(solution)/shard_map/pallas_call | solution.py:334
  119.7 2.0 %copy.9 = bf16[512,640]{1,0:T(8,128)(2,1)} copy(bf16[512,640]{1,0:T(8,128)(2,1)} %shard_map.73) | data formatting | bytes 1310720

commit v2 on v1

--- a/solution.py
+++ b/solution.py
@@ -48,7 +48,7 @@
 
 
 def kernel(table, docs, bq, bkv, tokens, wq_hbm, wkv_hbm, out,
-           tok, send, xg, wq, wraw, wkv, acc, qs, kv, pb, m_ref, l_ref, o_ref, on, stage,
+           tok, send, xg, wq, wraw, wkv, acc, qs, kv, pb, m_ref, l_ref, o_ref, stage,
            kpos, qlo, qhi, qplace,
            local_sem, a2a_send, a2a_recv, xs_send, x_recv, rl_send, rl_recv,
            kv_send, kv_recv, pb_send, pb_recv):
@@ -58,6 +58,7 @@
     my_y, my_z = lax.div(me, Z * C), lax.rem(lax.div(me, C), Z)
     right, left = lax.rem(x + 1, X), lax.rem(x + X - 1, X)
     onward = lax.rem(me + C, N)
+    onward2 = lax.rem(me + 2 * C, N)
     partner = me + 1 - 2 * core
 
     load_tok = pltpu.make_async_copy(tokens, tok, local_sem.at[0])
@@ -135,9 +136,9 @@
 
     def kv_copy(g, h):
         return pltpu.make_async_remote_copy(
-            src_ref=kv.at[h, g], dst_ref=kv.at[h + 1, g],
+            src_ref=kv.at[min(h, 1), g], dst_ref=kv.at[h + 1, g],
             send_sem=kv_send.at[h, g], recv_sem=kv_recv.at[h, g],
-            device_id=(onward, x), device_id_type=MESH)
+            device_id=(onward2 if h == 2 else onward, x), device_id_type=MESH)
 
     def pb_copy(g, i):
         return pltpu.make_async_remote_copy(
@@ -150,11 +151,16 @@
         x_send(g, 0).start()
         x_send(g, 1).start()
 
-    def chain(g, h):
-        kv_copy(g, h - 1).wait_recv()
-        if h < 3:
-            kv_copy(g, h).start()
-        pb_copy(g, h - 1).start()
+    def pass_on(g):
+        kv_copy(g, 0).wait_recv()
+        kv_copy(g, 1).start()
+        kv_copy(g, 2).start()
+        pb_copy(g, 0).start()
+
+    def share(g):
+        for h in (1, 2):
+            kv_copy(g, h).wait_recv()
+            pb_copy(g, h).start()
 
     def chain_end(g):
         for i in range(3):
@@ -176,6 +182,7 @@
     lane_slot = iota((1, SHARD), 1) >> 3
     lane_token = (iota((1, SHARD), 1) & 7).astype(jnp.float32)
     pair = iota((N // 2, 1), 0)
+    eye = iota((ROWS, ROWS), 0) == iota((ROWS, ROWS), 1)
     for buf, distance in enumerate(DISTANCES):
         shard = me - distance
         wrapped = shard & (N - 1)
@@ -187,18 +194,13 @@
         place = jnp.sum(jnp.where(hit, jnp.where((sender & 1) == 0, even, odd), 0.0), axis=0, keepdims=True)
         row = (shard * SHARD).astype(jnp.float32) + place * BLOCK + lane_token
         for g in range(G):
-            kpos[g, 0:1, buf * ROWS:(buf + 1) * ROWS] = row[:, g * ROWS:(g + 1) * ROWS]
+            across = jnp.where(eye, row[:, g * ROWS:(g + 1) * ROWS], 0.0)
+            kpos[g, buf * ROWS:(buf + 1) * ROWS, :] = jnp.sum(across, axis=1, keepdims=True)
+            if buf == 0:
+                qhi[g] = row[:, g * ROWS:(g + 1) * ROWS]
         if buf == 0:
-            mate = (lane >> 1) == pair
-            place_row = jnp.sum(jnp.where(mate, jnp.where((lane & 1) == 0, even, odd), 0.0), axis=0, keepdims=True)
-            row_index = iota((SHARD, 1), 0)
-            mine_from = sender_of(me, row_index >> 3)
-            place_col = jnp.sum(jnp.where(lane == mine_from, place_row, 0.0), axis=1, keepdims=True)
-            position = place_col * BLOCK + (row_index & 7).astype(jnp.float32)
             qplace[...] = row - (shard * SHARD).astype(jnp.float32)
-            here = (shard * SHARD).astype(jnp.float32) + position
-            for g in range(G):
-                qhi[g] = here[g * ROWS:(g + 1) * ROWS]
+            own_place = place
 
     my_docs = docs[pl.ds(lax.div(me, 2), 1), :].astype(jnp.float32)
     at = iota((N, 1), 0)
@@ -209,10 +211,9 @@
 
     counted = lax.fori_loop(0, 32, count, jnp.zeros((N, 128), jnp.float32))
     start_col = jnp.sum(counted, axis=1, keepdims=True) * BLOCK
-    start_row = jnp.sum(jnp.where(lane == at, start_col, 0.0), axis=0, keepdims=True)
-    low = jnp.sum(jnp.where(lane.astype(jnp.float32) == place_col, start_row, 0.0), axis=1, keepdims=True)
+    low = jnp.sum(jnp.where(own_place == at.astype(jnp.float32), start_col, 0.0), axis=0, keepdims=True)
     for g in range(G):
-        qlo[g] = low[g * ROWS:(g + 1) * ROWS]
+        qlo[g] = low[:, g * ROWS:(g + 1) * ROWS]
 
     m_ref[...] = jnp.full_like(m_ref, NEG)
     l_ref[...] = jnp.zeros_like(l_ref)
@@ -243,77 +244,85 @@
 
         for h in range(HEADS):
             qs[g, pl.ds(h * ROWS, ROWS), :] = acc[:, h * HEAD_SIZE:(h + 1) * HEAD_SIZE].astype(jnp.bfloat16)
-        kv[0, g] = acc[:, QW:].astype(jnp.bfloat16)
+        kv[0, g] = jnp.concatenate(
+            [acc[:, QW:QW + HEAD_SIZE], acc[:, QW + HEAD_SIZE:].T], axis=1).astype(jnp.bfloat16)
         kv_copy(g, 0).start()
 
     def attend(i, j):
-        keys = jnp.concatenate(
-            [kv[h, j][:, :HEAD_SIZE] for h in range(4)] + [pb[h, j][:, :HEAD_SIZE] for h in range(3)], axis=0)
-        values = jnp.concatenate(
-            [kv[h, j][:, HEAD_SIZE:] for h in range(4)] + [pb[h, j][:, HEAD_SIZE:] for h in range(3)], axis=0)
+        blocks = [kv[h, j] for h in range(4)] + [pb[h, j] for h in range(3)]
+        keys = jnp.concatenate([block[:, :HEAD_SIZE] for block in blocks], axis=0)
+        values = jnp.concatenate([block[:, HEAD_SIZE:] for block in blocks], axis=1)
+        values = jnp.concatenate([values, jnp.ones((16, KEYS), jnp.bfloat16)], axis=0)
         place = kpos[j]
         bias = jnp.where((place <= qhi[i]) & (place >= qlo[i]), 0.0, NEG)
-        s = lax.dot_general(qs[i], keys, (((1,), (1,)), ((), ())), preferred_element_type=jnp.float32)
-        s = (s.reshape(HEADS, ROWS, KEYS) + bias[None]).reshape(HEADS * ROWS, KEYS)
+        s = lax.dot_general(keys, qs[i], (((1,), (1,)), ((), ())), preferred_element_type=jnp.float32)
+        s = s + jnp.concatenate([bias] * HEADS, axis=1)
         m_old = m_ref[i]
-        m_new = jnp.maximum(m_old, jnp.max(s, axis=1, keepdims=True))
-        p = jnp.exp2((s - m_new[:, :1]) * SCALE)
+        m_new = jnp.maximum(m_old, jnp.max(s, axis=0, keepdims=True))
+        p = jnp.exp2((s - m_new) * SCALE).astype(jnp.bfloat16)
         alpha = jnp.exp2((m_old - m_new) * SCALE)
-        l_ref[i] = l_ref[i] * alpha + jnp.sum(p, axis=1, keepdims=True)
-        o_ref[i] = o_ref[i] * alpha + jnp.dot(p.astype(jnp.bfloat16), values, preferred_element_type=jnp.float32)
+        added = jnp.dot(values, p, preferred_element_type=jnp.float32)
+        o_ref[i] = o_ref[i] * alpha + added[:HEAD_SIZE]
+        l_ref[i] = l_ref[i] * alpha + added[HEAD_SIZE:HEAD_SIZE + 1]
         m_ref[i] = m_new
 
     group_ready(0)
     load_wq.wait()
-
-    @pl.loop(0, G + 2)
+    group_ready(1)
+
+    @pl.loop(0, G + 3)
     def _(step):
-        @pl.when(step >= 2)
-        def _():
-            j = step - 2
-            chain_end(j)
-            rows_there = jnp.minimum(step, G)
-            older = jnp.where(step <= G, j, 0)
-
-            @pl.loop(0, rows_there + older)
+        @pl.when(step < G)
+        def _():
+            for side in range(2):
+                x_send(step, side).wait_recv()
+                relay(step, side).start()
+
+        @pl.when(step + 2 < G)
+        def _():
+            group_ready(step + 2)
+
+        @pl.when((step >= 2) & (step <= G))
+        def _():
+            pass_on(step - 2)
+
+        @pl.when((step >= 1) & (step <= G))
+        def _():
+            project(step - 1)
+
+        @pl.when(step >= 3)
+        def _():
+            chain_end(step - 3)
+
+        j = step - 3
+        there = jnp.minimum(step, G)
+        pairs = jnp.where(step < 3, 0, there + jnp.where(step <= G, j, 0))
+
+        @pl.loop(0, 3)
+        def _(third):
+            @pl.when((third == 2) & (step == G))
+            def _():
+                pass_on(step - 1)
+
+            @pl.when((third == 2) & (step == G + 1))
+            def _():
+                share(step - 2)
+
+            @pl.loop(lax.div(pairs * third, 3), lax.div(pairs * (third + 1), 3))
             def _(t):
-                i = jnp.where(t < rows_there, t, rows_there - 1)
-                jj = jnp.where(t < rows_there, j, t - rows_there)
-                attend(i, jj)
-
-        @pl.when(step < G)
-        def _():
-            x_send(step, 0).wait_recv()
-            relay(step, 0).start()
-            x_send(step, 1).wait_recv()
-            relay(step, 1).start()
-
-        @pl.when(step + 1 < G)
-        def _():
-            group_ready(step + 1)
-
-        @pl.when((step >= 1) & (step <= G))
-        def _():
-            chain(step - 1, 1)
-
-        @pl.when(step < G)
-        def _():
-            project(step)
-
-        @pl.when((step >= 1) & (step <= G))
-        def _():
-            chain(step - 1, 2)
-            chain(step - 1, 3)
-
-    @pl.loop(0, G)
-    def _(g):
-        for h in range(HEADS):
-            rows = pl.ds(h * ROWS, ROWS)
-            part = o_ref[g, rows, :] / l_ref[g, rows, :]
-            on[pl.ds(g * ROWS, ROWS), h * HEAD_SIZE:(h + 1) * HEAD_SIZE] = part.astype(jnp.bfloat16)
+                attend(jnp.where(t < there, t, there - 1), jnp.where(t < there, j, t - there))
+
+        @pl.when((step >= 2) & (step <= G))
+        def _():
+            share(step - 2)
 
     order = jnp.where(iota((SHARD, 1), 0).astype(jnp.float32) == qplace[...], 1.0, 0.0).astype(jnp.bfloat16)
-    out[...] = jnp.dot(order, on[...], preferred_element_type=jnp.float32).astype(jnp.bfloat16)
+    for h in range(HEADS):
+        columns = slice(h * HEAD_SIZE, (h + 1) * HEAD_SIZE)
+        part = jnp.concatenate([o_ref[g, :, columns] / l_ref[g, :, columns] for g in range(G)], axis=1)
+        out[:, columns] = lax.dot_general(
+            order, part.astype(jnp.bfloat16), (((1,), (1,)), ((), ())), preferred_element_type=jnp.float32
+        ).astype(jnp.bfloat16)
 
     pltpu.make_async_copy(send.at[pl.ds(1, N - 1)], send.at[pl.ds(1, N - 1)], a2a_send).wait()
 
@@ -347,14 +356,13 @@
             pltpu.VMEM((G, HEADS * ROWS, HEAD_SIZE), bf16),
             pltpu.VMEM((4, G, ROWS, 2 * HEAD_SIZE), bf16),
             pltpu.VMEM((3, G, ROWS, 2 * HEAD_SIZE), bf16),
-            pltpu.VMEM((G, HEADS * ROWS, HEAD_SIZE), f32),
-            pltpu.VMEM((G, HEADS * ROWS, HEAD_SIZE), f32),
-            pltpu.VMEM((G, HEADS * ROWS, HEAD_SIZE), f32),
-            pltpu.VMEM((SHARD, QW), bf16),
+            pltpu.VMEM((G, 1, HEADS * ROWS), f32),
+            pltpu.VMEM((G, 1, HEADS * ROWS), f32),
+            pltpu.VMEM((G, HEAD_SIZE, HEADS * ROWS), f32),
             pltpu.VMEM((512, HEAD_SIZE), f32),
-            pltpu.VMEM((G, 1, KEYS), f32),
-            pltpu.VMEM((G, ROWS, 1), f32),
-            pltpu.VMEM((G, ROWS, 1), f32),
+            pltpu.VMEM((G, KEYS, 1), f32),
+            pltpu.VMEM((G, 1, ROWS), f32),
+            pltpu.VMEM((G, 1, ROWS), f32),
             pltpu.VMEM((1, SHARD), f32),
             dma((3,)), dma, dma((G,)),
             dma((2, G)), dma((2, G)), dma((2, G)), dma((2, G)),

time: 122 us -> 97.9 us (0.80)
  Pallas kernels: 120 us -> 95.8 us
    pallas_call x1, Pallas kernels: 120 us -> 95.8 us  [per_device(): pl.pallas_call(kernel, out_shape=jax.ShapeDtypeStruct((SHARD, QW), bf16),...]
where the time goes in v2:
time: 97.9 us; the launch traced here: 97.8 us
  Pallas kernels  95.8 us (98%)
  local copies, waits for them, and re-layouts  1.98 us (2%)
    pallas_call x1, Pallas kernels, per_device(): pl.pallas_call(kernel, out_shape=jax.ShapeDtypeStruct((SHARD, QW), bf16),...  95.8 us
    unnamed x1, local copies, waits for them, and re-layouts  1.98 us

profile of v2, /device:TPU:1, one launch (start us, length us, event | category | flops | bytes accessed | tf_op | source)
XLA Modules:
  0.0 97.8 jit_solution(11334701708569702570)
XLA Ops:
  0.0 95.8 %shard_map.73 = bf16[512,640]{1,0:T(8,128)(2,1)} custom-call(s32[32,128]{1,0:T(8,128)} %bitcast.5, s32[32,128]{1,0:T(8,128)} %bitcast.6, f32[5,128]{1,0:T(8,128)} %bitcast.7, f32[2,128]{1,0:T(2,128)} %bkv.1, bf16[512,1280]{1,0:T(8,128)(2,1)} %tokens.1, bf16[5120,640]{1,0:T(8,128)(2,1)} %wq_hbm.1, bf16[10240,128]{1,0:T(8,128)(2,1)} %bitcast.4), custom_call_target="tpu_custom_call" | custom-call | tf_op jit(solution)/shard_map/pallas_call | solution.py:343
  95.8 2.0 %copy.9 = bf16[512,640]{1,0:T(8,128)(2,1)} copy(bf16[512,640]{1,0:T(8,128)(2,1)} %shard_map.73) | data formatting | bytes 1310720

commit v3 on v2

--- a/solution.py
+++ b/solution.py
@@ -29,8 +29,9 @@
 
 
 def slot_parts(slot):
-    dz, dc = (slot >> 1) & (Z - 1), slot & 1
-    return ((slot >> 4) + dz) & (Y - 1), dz, dc
+    order = slot >> 3
+    dz = (((order + 1) >> 1) * (2 * (order & 1) - 1)) & (Z - 1)
+    return (slot >> 1) & (Y - 1), dz, slot & 1
 
 
 def sender_of(ctx, slot):
@@ -71,8 +72,9 @@
     barrier = pltpu.get_barrier_semaphore()
 
     def chip_at(u):
-        g, dz = lax.div(u, Z), lax.rem(u, Z)
-        return (lax.rem(my_y + lax.rem(g + dz, Y), Y) * Z + lax.rem(my_z + dz, Z)) * C
+        order, dy = lax.div(u, Y), lax.rem(u, Y)
+        dz = Z + lax.div(order + 1, 2) * (2 * lax.rem(order, 2) - 1)
+        return (lax.rem(my_y + dy, Y) * Z + lax.rem(my_z + dz, Z)) * C
 
     def cores_at(u):
         chip = chip_at(u)
@@ -94,6 +96,12 @@
     owners = jnp.broadcast_to((mine >> 6).astype(jnp.float32).astype(jnp.bfloat16), (8, 128))
     owner_of = jnp.dot(owners, spread, preferred_element_type=jnp.float32)[0:1].astype(jnp.int32)
     load_tok.wait()
+
+    def a2a(s, target):
+        return pltpu.make_async_remote_copy(
+            src_ref=send.at[s], dst_ref=xg.at[0, s], send_sem=a2a_send, recv_sem=a2a_recv.at[lax.div(s, PER)],
+            device_id=(target, x), device_id_type=MESH)
+
     for g in range(G):
         row = iota((ROWS, 1), 0)
         target = target_of(me, (row >> 3) + g * PER)
@@ -101,22 +109,15 @@
         picked = jnp.dot(jnp.where(pick, 1.0, 0.0).astype(jnp.bfloat16), tok[...], preferred_element_type=jnp.float32)
         halves = [picked[:, h * HALF:(h + 1) * HALF].reshape(PER, BLOCK, HALF) for h in range(2)]
         send[pl.ds(g * PER, PER)] = jnp.concatenate(halves, axis=1).astype(jnp.bfloat16)
-
-    pl.semaphore_wait(barrier, N + 1)
-
-    def a2a(s, target):
-        return pltpu.make_async_remote_copy(
-            src_ref=send.at[s], dst_ref=xg.at[0, s], send_sem=a2a_send, recv_sem=a2a_recv.at[lax.div(s, PER)],
-            device_id=(target, x), device_id_type=MESH)
-
-    own = pltpu.make_async_copy(send.at[0], xg.at[0, 0], a2a_recv.at[0])
-    own.start()
-    a2a(1, partner).start()
-
-    @pl.loop(1, N // 2)
-    def _(u):
-        for s, target in cores_at(u):
-            a2a(s, target).start()
+        if g == 0:
+            pl.semaphore_wait(barrier, N + 1)
+            pltpu.make_async_copy(send.at[0], xg.at[0, 0], a2a_recv.at[0]).start()
+            a2a(1, partner).start()
+
+        @pl.loop(max(1, g * PER // 2), (g + 1) * PER // 2)
+        def _(u):
+            for s, to in cores_at(u):
+                a2a(s, to).start()
 
     def group(g):
         return pl.ds(g * PER, PER)
@@ -165,6 +166,59 @@
     def chain_end(g):
         for i in range(3):
             pb_copy(g, i).wait_recv()
+
+    m_ref[...] = jnp.full_like(m_ref, NEG)
+    l_ref[...] = jnp.zeros_like(l_ref)
+    o_ref[...] = jnp.zeros_like(o_ref)
+
+    def project_part(g, part, peer):
+        piece = xg[part, group(g)].astype(jnp.float32)
+        lhs = jnp.concatenate(
+            [piece[:, :BLOCK].reshape(ROWS, HALF), piece[:, BLOCK:].reshape(ROWS, HALF)], axis=1
+        ).astype(jnp.bfloat16)
+        depth = pl.ds(pl.multiple_of(peer * DEPTH, DEPTH), DEPTH)
+        acc[:, :QW] += jnp.dot(lhs, wq[depth, :], preferred_element_type=jnp.float32)
+        acc[:, QW:] += jnp.dot(lhs, wkv[depth, :], preferred_element_type=jnp.float32)
+
+    def project(g):
+        acc[...] = jnp.concatenate(
+            [jnp.broadcast_to(b[h:h + 1, :], (ROWS, HEAD_SIZE)) for b in (bq, bkv) for h in range(b.shape[0])], axis=1)
+
+        @pl.loop(0, 4)
+        def _(part):
+            @pl.when(part == 3)
+            def _():
+                relay(g, 0).wait_recv()
+                relay(g, 1).wait_recv()
+
+            shift = jnp.where(part == 3, 2, jnp.where(part == 1, X - 1, jnp.where(part == 2, 1, 0)))
+            project_part(g, part, lax.rem(x + shift, X))
+
+        for h in range(HEADS):
+            qs[g, pl.ds(h * ROWS, ROWS), :] = acc[:, h * HEAD_SIZE:(h + 1) * HEAD_SIZE].astype(jnp.bfloat16)
+        kv[0, g] = jnp.concatenate(
+            [acc[:, QW:QW + HEAD_SIZE], acc[:, QW + HEAD_SIZE:].T], axis=1).astype(jnp.bfloat16)
+        kv_copy(g, 0).start()
+
+    def attend(i, j):
+        blocks = [kv[h, j] for h in range(4)] + [pb[h, j] for h in range(3)]
+        keys = jnp.concatenate([block[:, :HEAD_SIZE] for block in blocks], axis=0)
+        values = jnp.concatenate([block[:, HEAD_SIZE:] for block in blocks], axis=1)
+        values = jnp.concatenate([values, jnp.ones((16, KEYS), jnp.bfloat16)], axis=0)
+        place = kpos[j]
+        bias = jnp.where((place <= qhi[i]) & (place >= qlo[i]), 0.0, NEG)
+        s = lax.dot_general(keys, qs[i], (((1,), (1,)), ((), ())), preferred_element_type=jnp.float32)
+        s = s + jnp.concatenate([bias] * HEADS, axis=1)
+        m_old = m_ref[i]
+        m_new = jnp.maximum(m_old, jnp.max(s, axis=0, keepdims=True))
+        p = jnp.exp2((s - m_new) * SCALE).astype(jnp.bfloat16)
+        alpha = jnp.exp2((m_old - m_new) * SCALE)
+        added = jnp.dot(values, p, preferred_element_type=jnp.float32)
+        o_ref[i] = o_ref[i] * alpha + added[:HEAD_SIZE]
+        l_ref[i] = l_ref[i] * alpha + added[HEAD_SIZE:HEAD_SIZE + 1]
+        m_ref[i] = m_new
+
+    group_ready(0)
 
     load_wkv.wait()
 
@@ -215,60 +269,8 @@
     for g in range(G):
         qlo[g] = low[:, g * ROWS:(g + 1) * ROWS]
 
-    m_ref[...] = jnp.full_like(m_ref, NEG)
-    l_ref[...] = jnp.zeros_like(l_ref)
-    o_ref[...] = jnp.zeros_like(o_ref)
-
-    def project_part(g, part, peer):
-        piece = xg[part, group(g)].astype(jnp.float32)
-        lhs = jnp.concatenate(
-            [piece[:, :BLOCK].reshape(ROWS, HALF), piece[:, BLOCK:].reshape(ROWS, HALF)], axis=1
-        ).astype(jnp.bfloat16)
-        depth = pl.ds(pl.multiple_of(peer * DEPTH, DEPTH), DEPTH)
-        acc[:, :QW] += jnp.dot(lhs, wq[depth, :], preferred_element_type=jnp.float32)
-        acc[:, QW:] += jnp.dot(lhs, wkv[depth, :], preferred_element_type=jnp.float32)
-
-    def project(g):
-        acc[...] = jnp.concatenate(
-            [jnp.broadcast_to(b[h:h + 1, :], (ROWS, HEAD_SIZE)) for b in (bq, bkv) for h in range(b.shape[0])], axis=1)
-
-        @pl.loop(0, 4)
-        def _(part):
-            @pl.when(part == 3)
-            def _():
-                relay(g, 0).wait_recv()
-                relay(g, 1).wait_recv()
-
-            shift = jnp.where(part == 3, 2, jnp.where(part == 1, X - 1, jnp.where(part == 2, 1, 0)))
-            project_part(g, part, lax.rem(x + shift, X))
-
-        for h in range(HEADS):
-            qs[g, pl.ds(h * ROWS, ROWS), :] = acc[:, h * HEAD_SIZE:(h + 1) * HEAD_SIZE].astype(jnp.bfloat16)
-        kv[0, g] = jnp.concatenate(
-            [acc[:, QW:QW + HEAD_SIZE], acc[:, QW + HEAD_SIZE:].T], axis=1).astype(jnp.bfloat16)
-        kv_copy(g, 0).start()
-
-    def attend(i, j):
-        blocks = [kv[h, j] for h in range(4)] + [pb[h, j] for h in range(3)]
-        keys = jnp.concatenate([block[:, :HEAD_SIZE] for block in blocks], axis=0)
-        values = jnp.concatenate([block[:, HEAD_SIZE:] for block in blocks], axis=1)
-        values = jnp.concatenate([values, jnp.ones((16, KEYS), jnp.bfloat16)], axis=0)
-        place = kpos[j]
-        bias = jnp.where((place <= qhi[i]) & (place >= qlo[i]), 0.0, NEG)
-        s = lax.dot_general(keys, qs[i], (((1,), (1,)), ((), ())), preferred_element_type=jnp.float32)
-        s = s + jnp.concatenate([bias] * HEADS, axis=1)
-        m_old = m_ref[i]
-        m_new = jnp.maximum(m_old, jnp.max(s, axis=0, keepdims=True))
-        p = jnp.exp2((s - m_new) * SCALE).astype(jnp.bfloat16)
-        alpha = jnp.exp2((m_old - m_new) * SCALE)
-        added = jnp.dot(values, p, preferred_element_type=jnp.float32)
-        o_ref[i] = o_ref[i] * alpha + added[:HEAD_SIZE]
-        l_ref[i] = l_ref[i] * alpha + added[HEAD_SIZE:HEAD_SIZE + 1]
-        m_ref[i] = m_new
-
-    group_ready(0)
+    group_ready(1)
     load_wq.wait()
-    group_ready(1)
 
     @pl.loop(0, G + 3)
     def _(step):

time: 97.9 us -> 93.9 us (0.959)
  Pallas kernels: 95.8 us -> 91.7 us
    pallas_call x1, Pallas kernels: 95.8 us -> 91.7 us  [per_device(): pl.pallas_call(kernel, out_shape=jax.ShapeDtypeStruct((SHARD, QW), bf16),...]
where the time goes in v3:
time: 93.9 us; the launch traced here: 93.7 us
  Pallas kernels  91.7 us (98%)
  local copies, waits for them, and re-layouts  1.98 us (2%)
    pallas_call x1, Pallas kernels, per_device(): pl.pallas_call(kernel, out_shape=jax.ShapeDtypeStruct((SHARD, QW), bf16),...  91.7 us
    unnamed x1, local copies, waits for them, and re-layouts  1.98 us

profile of v3, /device:TPU:1, one launch (start us, length us, event | category | flops | bytes accessed | tf_op | source)
XLA Modules:
  0.0 93.7 jit_solution(4986244487233614269)
XLA Ops:
  0.0 91.7 %shard_map.73 = bf16[512,640]{1,0:T(8,128)(2,1)} custom-call(s32[32,128]{1,0:T(8,128)} %bitcast.5, s32[32,128]{1,0:T(8,128)} %bitcast.6, f32[5,128]{1,0:T(8,128)} %bitcast.7, f32[2,128]{1,0:T(2,128)} %bkv.1, bf16[512,1280]{1,0:T(8,128)(2,1)} %tokens.1, bf16[5120,640]{1,0:T(8,128)(2,1)} %wq_hbm.1, bf16[10240,128]{1,0:T(8,128)(2,1)} %bitcast.4), custom_call_target="tpu_custom_call" | custom-call | tf_op jit(solution)/shard_map/pallas_call | solution.py:345
  91.7 2.0 %copy.9 = bf16[512,640]{1,0:T(8,128)(2,1)} copy(bf16[512,640]{1,0:T(8,128)(2,1)} %shard_map.73) | data formatting | bytes 1310720

commit v4 on v3

--- a/solution.py
+++ b/solution.py
@@ -280,25 +280,33 @@
                 x_send(step, side).wait_recv()
                 relay(step, side).start()
 
+        @pl.when((step >= 3) & (step <= G))
+        def _():
+            pass_on(step - 2)
+
+        @pl.when((step >= 1) & (step <= G))
+        def _():
+            project(step - 1)
+
         @pl.when(step + 2 < G)
         def _():
             group_ready(step + 2)
 
-        @pl.when((step >= 2) & (step <= G))
-        def _():
-            pass_on(step - 2)
-
-        @pl.when((step >= 1) & (step <= G))
-        def _():
-            project(step - 1)
-
-        @pl.when(step >= 3)
-        def _():
-            chain_end(step - 3)
-
-        j = step - 3
+        @pl.when(step == 1)
+        def _():
+            pass_on(0)
+
+        @pl.when(step == 2)
+        def _():
+            share(0)
+
+        @pl.when((step == 2) | (step >= 4))
+        def _():
+            chain_end(jnp.where(step == 2, 0, step - 3))
+
+        j = jnp.where(step <= 3, 0, step - 3)
         there = jnp.minimum(step, G)
-        pairs = jnp.where(step < 3, 0, there + jnp.where(step <= G, j, 0))
+        pairs = jnp.where(step < 2, 0, jnp.where(step == 2, 2, jnp.where(step == 3, 1, there + jnp.where(step <= G, j, 0))))
 
         @pl.loop(0, 3)
         def _(third):
@@ -312,9 +320,10 @@
 
             @pl.loop(lax.div(pairs * third, 3), lax.div(pairs * (third + 1), 3))
             def _(t):
-                attend(jnp.where(t < there, t, there - 1), jnp.where(t < there, j, t - there))
-
-        @pl.when((step >= 2) & (step <= G))
+                i = jnp.where(step == 3, 2, jnp.where(t < there, t, there - 1))
+                attend(i, jnp.where(t < there, j, t - there))
+
+        @pl.when((step >= 3) & (step <= G))
         def _():
             share(step - 2)
 

time: 93.9 us -> 93.4 us (level)
  no operation moved by 1% of the time
where the time goes in v4:
time: 93.4 us; the launch traced here: 92.9 us
  Pallas kernels  90.9 us (97%)
  local copies, waits for them, and re-layouts  1.98 us (2%)
    pallas_call x1, Pallas kernels, per_device(): pl.pallas_call(kernel, out_shape=jax.ShapeDtypeStruct((SHARD, QW), bf16),...  90.9 us
    unnamed x1, local copies, waits for them, and re-layouts  1.98 us

profile of v4, /device:TPU:1, one launch (start us, length us, event | category | flops | bytes accessed | tf_op | source)
XLA Modules:
  0.0 92.9 jit_solution(15778394357348609290)
XLA Ops:
  0.0 90.9 %shard_map.73 = bf16[512,640]{1,0:T(8,128)(2,1)} custom-call(s32[32,128]{1,0:T(8,128)} %bitcast.5, s32[32,128]{1,0:T(8,128)} %bitcast.6, f32[5,128]{1,0:T(8,128)} %bitcast.7, f32[2,128]{1,0:T(2,128)} %bkv.1, bf16[512,1280]{1,0:T(8,128)(2,1)} %tokens.1, bf16[5120,640]{1,0:T(8,128)(2,1)} %wq_hbm.1, bf16[10240,128]{1,0:T(8,128)(2,1)} %bitcast.4), custom_call_target="tpu_custom_call" | custom-call | tf_op jit(solution)/shard_map/pallas_call | solution.py:354
  90.9 2.0 %copy.9 = bf16[512,640]{1,0:T(8,128)(2,1)} copy(bf16[512,640]{1,0:T(8,128)(2,1)} %shard_map.73) | data formatting | bytes 1310720

commit v5 on v4

--- a/solution.py
+++ b/solution.py
@@ -312,6 +312,7 @@
         def _(third):
             @pl.when((third == 2) & (step == G))
             def _():
+                share(step - 2)
                 pass_on(step - 1)
 
             @pl.when((third == 2) & (step == G + 1))
@@ -323,7 +324,7 @@
                 i = jnp.where(step == 3, 2, jnp.where(t < there, t, there - 1))
                 attend(i, jnp.where(t < there, j, t - there))
 
-        @pl.when((step >= 3) & (step <= G))
+        @pl.when(step == 3)
         def _():
             share(step - 2)
 

time: 93.4 us -> 93.6 us (level)
  no operation moved by 1% of the time
where the time goes in v5:
time: 93.6 us; the launch traced here: 93.4 us
  Pallas kernels  91.4 us (98%)
  local copies, waits for them, and re-layouts  1.98 us (2%)
    pallas_call x1, Pallas kernels, per_device(): pl.pallas_call(kernel, out_shape=jax.ShapeDtypeStruct((SHARD, QW), bf16),...  91.4 us
    unnamed x1, local copies, waits for them, and re-layouts  1.98 us

profile of v5, /device:TPU:1, one launch (start us, length us, event | category | flops | bytes accessed | tf_op | source)
XLA Modules:
  0.0 93.4 jit_solution(12171643554530736670)
XLA Ops:
  0.0 91.4 %shard_map.73 = bf16[512,640]{1,0:T(8,128)(2,1)} custom-call(s32[32,128]{1,0:T(8,128)} %bitcast.5, s32[32,128]{1,0:T(8,128)} %bitcast.6, f32[5,128]{1,0:T(8,128)} %bitcast.7, f32[2,128]{1,0:T(2,128)} %bkv.1, bf16[512,1280]{1,0:T(8,128)(2,1)} %tokens.1, bf16[5120,640]{1,0:T(8,128)(2,1)} %wq_hbm.1, bf16[10240,128]{1,0:T(8,128)(2,1)} %bitcast.4), custom_call_target="tpu_custom_call" | custom-call | tf_op jit(solution)/shard_map/pallas_call | solution.py:355
  91.4 2.0 %copy.9 = bf16[512,640]{1,0:T(8,128)(2,1)} copy(bf16[512,640]{1,0:T(8,128)(2,1)} %shard_map.73) | data formatting | bytes 1310720
